TPU v7x, 512 devices: a whole 4x4x16 slice. The times are simulated.
512 devices in a mesh: lat: 4 (over x), lon: 32 (over z, core), lev: 4 (over y).
Axes of the slice: x: 4, y: 4, z: 16, core: 2. Of those that a mesh axis runs over, the one named last changes fastest.
Arguments:
- fields: bfloat16 [24, 64, 40960], P('lev', 'lon', 'lat'), may hold values from -6 to 6
- slot_level: int32 [24], P('lev'), may hold values from -1 to 13, as said below
- embed_weight: bfloat16 [80, 512], replicated, may hold values from -0.625 to 0.625
- level_encoding: bfloat16 [14, 512], replicated, may hold values from -6 to 6
- latent_queries: bfloat16 [3, 512], replicated, may hold values from -400 to 400
- qkv_weight: bfloat16 [3, 512, 512], P(None, ('lon', 'lev')), may hold values from -0.25 to 0.25
- out_weight: bfloat16 [512, 512], P(('lon', 'lev')), may hold values from -0.25 to 0.25
Outputs:
- latents: bfloat16 [3, 512, 64, 512], P(None, ('lat', 'lon', 'lev'))
Inputs may be any that keep to these rules, and one draw needn't show every extreme that they name: `slot_level`: each lev device's 6 slots hold its levels first and -1 after them; every device holds 1 to 6 levels, some device exactly 6; every level 0 to 13 is held by exactly one slot.
All inputs are finite; a program needn't handle non-finite values.
Results may differ from a plain program's by a relative error of at most 0.013.
The roundings to bfloat16 on the way count: a program that leaves them out, or rounds other values in their place, can miss the bound.
Values may be sent and summed in bfloat16 or wider, within the bound.
A program may use at most 64 MiB of HBM per device.

v0:
```python
import math

import jax
import jax.numpy as jnp
from jax import lax
from jax.sharding import PartitionSpec as P

HEADS = 16


def joined(part, axis, combine):
    gathered = jax.tree.map(lambda a: lax.all_gather(a, axis), part)

    def take(source):
        return jax.tree.map(lambda a: lax.dynamic_index_in_dim(a, source, 0, False), gathered)

    return lax.fori_loop(
        1, lax.axis_size(axis), lambda source, state: combine(state, take(source)), take(0)
    )


def rescale(weighted, factor):
    return (weighted.reshape(factor.shape + (-1,)) * factor[..., None]).reshape(weighted.shape)


def combine(first_part, second_part):
    highest_a, summed_a, weighted_a = first_part
    highest_b, summed_b, weighted_b = second_part
    highest = jnp.maximum(highest_a, highest_b)
    factor_a = jnp.exp(highest_a - highest)
    factor_b = jnp.exp(highest_b - highest)
    summed = summed_a * factor_a + summed_b * factor_b
    weighted = rescale(weighted_a, factor_a) + rescale(weighted_b, factor_b)
    return (highest, summed, weighted)


def attend(patch_rows, level_of, count, weights, query_heads, embed_weight, level_encoding):
    latent_count, head_count, head_dim = query_heads.shape
    width_model = weights.shape[2]
    patch_count = patch_rows.shape[1]
    level_count = level_encoding.shape[0]
    kv_weight = weights[1:3].reshape(2 * width_model, width_model)
    scale_factor = 1.0 / math.sqrt(head_dim)
    start_state = (
        jnp.full((latent_count, head_count, patch_count), -1e30, jnp.float32),
        jnp.zeros((latent_count, head_count, patch_count), jnp.float32),
        jnp.zeros((latent_count, head_count, patch_count * head_dim), jnp.float32),
    )

    def step(position, state):
        highest_old, summed_old, weighted_old = state
        slot_rows = lax.dynamic_index_in_dim(patch_rows, position, 0, keepdims=False)
        level = lax.dynamic_index_in_dim(level_of, position, 0, keepdims=False)
        one_hot = (jnp.arange(level_count, dtype=jnp.int32) == level).astype(jnp.bfloat16)
        encoding = jnp.dot(one_hot[None, :], level_encoding, preferred_element_type=jnp.float32)
        embedded = (
            jnp.dot(slot_rows, embed_weight, preferred_element_type=jnp.float32) + encoding
        ).astype(jnp.bfloat16)
        projected = lax.dot_general(
            embedded, kv_weight, (((1,), (1,)), ((), ())), preferred_element_type=jnp.float32
        ).astype(jnp.bfloat16)
        keys = projected[:, :width_model].reshape(patch_count, head_count, head_dim)
        values = projected[:, width_model:].reshape(patch_count, head_count, head_dim)
        scores = (
            jnp.einsum("ahj,phj->ahp", query_heads, keys, preferred_element_type=jnp.float32)
            * scale_factor
        )
        highest = jnp.maximum(highest_old, scores)
        decay = jnp.exp(highest_old - highest)
        expo = jnp.exp(scores - highest)
        value_heads = jnp.transpose(values, (1, 0, 2))
        addition = (expo[..., None] * value_heads[None]).reshape(
            latent_count, head_count, patch_count * head_dim
        )
        weighted = rescale(weighted_old, decay) + addition
        return (highest, summed_old * decay + expo, weighted)

    return lax.fori_loop(0, count, step, start_state)


def on_device(
    fields, slot_level, embed_weight, level_encoding, latent_queries, qkv_weight, out_weight
):
    slots, lon_patches, lat_width = fields.shape
    in_width = embed_weight.shape[0]
    width_model = embed_weight.shape[1]
    latent_count = latent_queries.shape[0]
    head_dim = width_model // HEADS
    lat_patches = lat_width // in_width
    lon_count = lax.axis_size("lon")
    lev_count = lax.axis_size("lev")
    out_rows = lat_patches // (lon_count * lev_count)
    weights = lax.all_gather(qkv_weight, ("lon", "lev"), axis=1, tiled=True)
    queries = lax.dot_general(
        latent_queries, weights[0], (((1,), (1,)), ((), ())), preferred_element_type=jnp.float32
    ).astype(jnp.bfloat16)
    query_heads = queries.reshape(latent_count, HEADS, head_dim)
    patch_rows = fields.reshape(slots, lon_patches * lat_patches, in_width)
    live_count = jnp.sum((slot_level >= 0).astype(jnp.int32))
    highest, summed, weighted = attend(
        patch_rows, slot_level, live_count, weights, query_heads, embed_weight, level_encoding
    )
    highest, summed, weighted = joined((highest, summed, weighted), "lev", combine)
    grid_shape = (latent_count, HEADS, lon_patches, lon_count, lev_count, out_rows)
    mixed = (
        weighted.reshape(grid_shape + (head_dim,)) / summed.reshape(grid_shape)[..., None]
    ).astype(jnp.bfloat16)
    ordered = jnp.transpose(mixed, (0, 3, 4, 5, 2, 1, 6)).reshape(-1, width_model)
    projected = lax.dot_general(
        ordered,
        lax.all_gather(out_weight, ("lon", "lev"), axis=0, tiled=True),
        (((1,), (1,)), ((), ())),
        preferred_element_type=jnp.float32,
    ).astype(jnp.bfloat16)
    blocks = projected.reshape(
        latent_count, lon_count, lev_count, out_rows, lon_patches, width_model
    )
    regrouped = lax.all_to_all(blocks, "lon", split_axis=1, concat_axis=4, tiled=True)
    regrouped = lax.dynamic_index_in_dim(regrouped, lax.axis_index("lev"), 2, keepdims=True)
    return regrouped.reshape(latent_count, out_rows, lon_count * lon_patches, width_model)


def solution(mesh):
    in_specs = (
        P("lev", "lon", "lat"),
        P("lev"),
        P(),
        P(),
        P(),
        P(None, ("lon", "lev"), None),
        P(("lon", "lev"), None),
    )
    out_specs = P(None, ("lat", "lon", "lev"), None, None)
    return jax.shard_map(
        on_device, mesh=mesh, in_specs=in_specs, out_specs=out_specs, check_vma=False
    )
```

profile of v0, /device:TPU:1, one launch (start us, length us, event | category | flops | bytes accessed | tf_op | source)
XLA Modules:
  0.0 662.0 jit_solution(10881343465634277629)
XLA Ops:
  6.5 1.3 copy.59
  7.9 1.4 reshape.97
  9.4 1.3 fusion.19
  10.7 145.4 %all-gather.7.cloned.1.call-done = bf16[3,512,512]{2,0,1:T(4,128)(2,1)} async-done(((bf16[3,4,512]{2,0,1:T(4,128)(2,1)}), bf16[3,512,512]{2,0,1:T(4,128)(2,1)}) %all-gather.7.cloned.1.call-update) | async-done | bytes 1572880 | tf_op jit(solution)/shard_map/all_gather | solution.py:93
  156.0 2.9 slice.22
  159.0 1.1 copy.72
  161.3 1.2 broadcast_in_dim.21
  162.5 59.5 %while.33 = (s32[]{:T(128)}, f32[3,16,256]{2,0,1:T(4,128)S(1)}, f32[3,16,256]{2,0,1:T(4,128)S(1)}, f32[3,16,8192]{2,1,0:T(8,128)}, s32[]{:T(128)}, /*index=5*/bf...) while((s32[]{:T(128)}, f32[3,16,256]{2,0,1:T(4,128)S(1)}, ...), condition=%wide.region_2.3_spmd, body=%wide.region_1.2_spmd.sunk | while | flops 292116512 | bytes 23827652 | solution.py:78
  164.4 1.8 convolution_convert_fusion.4
  166.6 3.8 mul.149
  170.4 6.1 mul.150
  176.5 3.8 mul.151
  180.3 6.1 mul.152
  187.2 1.0 reshape.120
  188.2 3.8 multiply_add_fusion.5
  193.9 1.8 convolution_convert_fusion.4
  196.1 3.8 mul.149
  199.9 6.1 mul.150
  206.0 3.8 mul.151
  209.7 6.1 mul.152
  217.6 3.8 multiply_add_fusion.5
  222.7 261.5 %all-gather.3 = bf16[128,4,512]{2,1,0:T(4,128)(2,1)S(1)} all-gather(bf16[1,4,512]{2,1,0:T(4,128)(2,1)S(1)} %bitcast.104), channel_id=1, replica_groups=mesh['lat'=4,'lon'=32,'lev'=4] {'lon','lev'}, dimensions={0}, use_global_device_ids=true | all-gather | bytes 528384 | tf_op jit(solution)/shard_map/all_gather | solution.py:111
  485.1 9.2 %all-gather = f32[12,16,256]{2,1,0:T(8,128)S(1)} all-gather(f32[3,16,256]{2,1,0:T(8,128)S(1)} %copy.63), channel_id=2, replica_groups=mesh['lat'=4,'lon'=32,'lev'=4] {'lev'}, dimensions={0}, use_global_device_ids=true | all-gather | bytes 245760 | tf_op jit(solution)/shard_map/all_gather | solution.py:12
  494.4 10.2 %all-gather.1 = f32[12,16,256]{2,1,0:T(8,128)} all-gather(f32[3,16,256]{2,1,0:T(8,128)S(1)} %copy.64), channel_id=3, replica_groups=mesh['lat'=4,'lon'=32,'lev'=4] {'lev'}, dimensions={0}, use_global_device_ids=true | all-gather | bytes 245760 | tf_op jit(solution)/shard_map/all_gather | solution.py:12
  505.3 2.7 slice.26
  508.0 67.3 %while.34 = (s32[]{:T(128)}, f32[3,16,256]{2,1,0:T(8,128)S(1)}, f32[3,16,256]{2,1,0:T(8,128)S(1)}, f32[3,16,8192]{2,1,0:T(8,128)}, f32[4,3,16,256]{3,2,1,0:T(8,1...) while((s32[]{:T(128)}, f32[3,16,256]{2,1,0:T(8,128)S(1)}, ...), condition=%wide.region_4.5_spmd, body=%wide.region_3.4_spmd.sunk | while | flops 1253381 | bytes 17793176 | solution.py:17
  508.9 3.9 mul.157
  512.7 5.1 mul.158
  517.8 3.9 mul.159
  521.7 5.1 mul.160
  526.8 3.6 fusion.48
  531.3 3.9 mul.157
  535.2 5.1 mul.158
  540.3 3.9 mul.159
  544.1 5.1 mul.160
  549.2 3.6 fusion.48
  553.7 3.9 mul.157
  557.6 5.1 mul.158
  562.7 3.9 mul.159
  566.6 5.1 mul.160
  571.7 3.6 fusion.48
  575.8 6.0 reshape.100
  581.8 6.7 %fusion.18 = bf16[3,32,4,1,2,16,32]{6,5,4,2,1,0,3:T(8,128)(2,1)S(1)} fusion(f32[3,16,2,32,4]{1,2,4,3,0:T(2,128)S(1)} %copy.66, f32[3,16,2,32,4,1,32]{6,4,3,2,1,0,5:T(4,128)} %reshape.100), kind=kLoop, calls=%fused_computation.29 | loop fusion | flops 786432 | bytes 2408448 | tf_op jit(solution)/shard_map/transpose | solution.py:108
  588.5 3.9 reshape.101
  592.4 1.9 convolution_convert_fusion.1
  594.6 1.2 copy.68
  595.8 13.3 %all-to-all-start = ((bf16[3,32,4,1,2,512]{5,2,4,0,3,1:T(4,128)(2,1)}), bf16[3,32,4,1,2,512]{5,2,4,0,3,1:T(4,128)(2,1)S(1)}, u32[]{:S(2)}, u32[]{:S(2)}) async-start(bf16[3,32,4,1,2,512]{5,2,4,0,3,1:T(4,128)(2,1)} %copy.68), calls=%async_computation | async-start | bytes 1572864 | tf_op jit(solution)/shard_map/all_to_all | solution.py:118
  609.1 44.6 %all-to-all-done = bf16[3,32,4,1,2,512]{5,2,4,0,3,1:T(4,128)(2,1)S(1)} async-done(((bf16[3,32,4,1,2,512]{5,2,4,0,3,1:T(4,128)(2,1)}), bf16[3,32,4,1,2,512]{5,2,4,0,3,1:T(4,128)(2,1)S(1)}, u32[]{:S(2)}, u32[]{:S(2)}) %all-to-all-start) | async-done | bytes 786464 | tf_op jit(solution)/shard_map/all_to_all | solution.py:118
  (58 shorter events, 14.4 us)
Async XLA Ops:
  6.5 154.3 %copy-start = (bf16[3,512]{1,0:T(4,128)(2,1)S(1)}, bf16[3,512]{1,0:T(4,128)(2,1)}, u32[]{:S(2)}) copy-start(bf16[3,512]{1,0:T(4,128)(2,1)} %param.15) | copy-start | bytes 9220
  6.5 149.5 %all-gather.7.cloned.1.call-start = ((), (), s32[]{:S(2)}) async-start(), calls=%async_computation.1 | async-start | bytes 2113536 | tf_op jit(solution)/shard_map/all_gather | solution.py:93
  7.9 497.4 %all-gather.9.cloned.1.call-start = ((), (), s32[]{:S(2)}) async-start(), calls=%async_computation.2 | async-start | bytes 7864320 | tf_op jit(solution)/shard_map/all_gather | solution.py:12
  156.0 4.1 copy-start.2
  160.8 1.7 copy-start.3
  160.8 1.7 copy-start.5
  160.9 1.6 copy-start.6
  222.0 0.7 copy-start.4
  595.8 57.9 %all-to-all-start = ((bf16[3,32,4,1,2,512]{5,2,4,0,3,1:T(4,128)(2,1)}), bf16[3,32,4,1,2,512]{5,2,4,0,3,1:T(4,128)(2,1)S(1)}, u32[]{:S(2)}, u32[]{:S(2)}) async-start(bf16[3,32,4,1,2,512]{5,2,4,0,3,1:T(4,128)(2,1)} %copy.68), calls=%async_computation | async-start | bytes 1572864 | tf_op jit(solution)/shard_map/all_to_all | solution.py:118
  609.1 46.1 %copy-start.1 = (bf16[3,512]{1,0:T(4,128)(2,1)S(1)}, bf16[3,512]{1,0:T(4,128)(2,1)}, u32[]{:S(2)}) copy-start(bf16[3,512]{1,0:T(4,128)(2,1)} %param.15) | copy-start | bytes 9220
Sparse Core Ops, SparseCore 0:
  10.5 145.4 all-gather.6
  222.1 185.4 all-gather.8
where the time goes:
time: 664 us; the launch traced here: 662 us
  blocking collectives  281 us (42%)
  waiting for transfers between devices  190 us (29%)
  local copies, waits for them, and re-layouts  126 us (19%)
  other arithmetic  29.1 us (4%)
  between operations  13.6 us (2%)
  starting transfers between devices  13.3 us (2%)
  matrix products  7.61 us (1%)
    all_gather x1, blocking collectives, on_device(): lax.all_gather(out_weight, ('lon', 'lev'), axis=0, tiled=True)  261 us
    all_gather x1, waiting for transfers between devices, on_device(): weights = lax.all_gather(qkv_weight, ('lon', 'lev'), axis=1, tiled=True)  145 us
    mul x16, local copies, waits for them, and re-layouts, rescale(): weighted.reshape(factor.shape + (-1,)) * factor[..., None]  73.6 us
    all_to_all x1, waiting for transfers between devices, on_device(): lax.all_to_all(blocks, 'lon', split_axis=1, concat_axis=4, tiled=True)  44.6 us
    mul x10, local copies, waits for them, and re-layouts, step(): expo[..., None] * value_heads[None]  23.2 us
    all_gather x2, blocking collectives, joined(): gathered = jax.tree.map(lambda a: lax.all_gather(a, axis), part)  19.4 us
  transfers between devices with their start and end apart: 3, of which 2 were waited for; matrix products, arithmetic and copies ran while one was open for 1% of the time, Pallas kernels for 0%

commit v1 on v0

v1 whole, which is shorter than its diff:
```python
import functools
import math

import jax
import jax.numpy as jnp
from jax import lax
from jax.experimental import pallas as pl
from jax.experimental.pallas import tpu as pltpu
from jax.sharding import PartitionSpec as P

MESH = pl.DeviceIdType.MESH
F32 = jnp.float32
BF16 = jnp.bfloat16
NZ, NY, NX, NC = 16, 4, 4, 2
IN = 80
D = 512
LEVELS = 14
HEADS = 16
LATENT = 3
UNITS = 8 * IN
ROW = NZ * IN
ROWL = ROW + 128


def iota(shape, dim):
    return lax.broadcasted_iota(jnp.int32, shape, dim)


def nt(a, b):
    return lax.dot_general(a, b, (((1,), (1,)), ((), ())), preferred_element_type=F32)


def far_first(t):
    half = (t + 1) // 2
    return 8 + half * (1 - 2 * (t % 2))


def exchange_kernel(
    fields, slot_level, latent, qkv, out_w,
    w_all, q_all, f_all,
    tile, wy, regroup, f0, fy, fs,
    wz_s, wz_r, wy_s, wy_r, wx_s, wx_r, wc_s, wc_r, fy_s, fy_r, fz_s, fz_r,
):
    x = lax.axis_index("lat")
    lon = lax.axis_index("lon")
    y = lax.axis_index("lev")
    z = lon // 2
    c = lon % 2

    def device(dx=0, dy=0, dz=0, dc=0):
        return {
            "lat": (x + dx) % NX,
            "lon": ((z + dz) % NZ) * 2 + (c + dc) % 2,
            "lev": (y + dy) % NY,
        }

    barrier = pltpu.get_barrier_semaphore()

    def greet(dev):
        pl.semaphore_signal(barrier, inc=1, device_id=dev, device_id_type=MESH)

    def greet_z(t, carry):
        greet(device(dz=t))
        return carry

    def greet_yc(t, carry):
        greet(device(dy=t // 2, dc=t % 2))
        return carry

    def greet_x(t, carry):
        greet(device(dx=t))
        return carry

    lax.fori_loop(1, NZ, greet_z, 0)
    lax.fori_loop(1, 8, greet_yc, 0)
    lax.fori_loop(1, NX, greet_x, 0)

    wq = qkv[0].astype(F32)
    lat = latent[...].astype(F32)
    lane = iota((4, 128), 1)
    q = jnp.zeros((4, 128), F32)
    for a in range(LATENT):
        col = jnp.sum(wq * lat[a : a + 1, :], axis=1, keepdims=True)
        q = jnp.where(lane == a, col, q)
    for part in range(NX):
        cut = slice(part * 128, part * 128 + 128)
        tile[part] = jnp.concatenate(
            [q, qkv[1, :, cut].astype(F32), qkv[2, :, cut].astype(F32), out_w[:, cut].astype(F32)], axis=0
        ).astype(BF16)

    for g in range(2):
        blocks = []
        for e in range(8):
            at = (8 * g + e) * UNITS
            rows = [fields[s, :, at : at + UNITS].astype(F32) for s in range(6)]
            blocks.append(jnp.concatenate(rows + [jnp.zeros((4, UNITS), F32)], axis=0))
        for d in range(8):
            f0[d, :, g * UNITS : (g + 1) * UNITS] = jnp.concatenate(
                [blocks[e][:, d * IN : (d + 1) * IN] for e in range(8)], axis=1
            ).astype(BF16)
    slot_of_row = iota((16, 128), 0) // 2
    levels = jnp.full((16, 128), -1.0, F32)
    for s in range(6):
        levels = jnp.where(slot_of_row == s, slot_level[s].astype(F32), levels)
    for d in range(8):
        f0[d, :, ROW:ROWL] = levels.astype(BF16)

    pl.semaphore_wait(barrier, NZ - 1 + 7 + NX - 1)

    def wz_copy(s):
        return pltpu.make_async_remote_copy(
            src_ref=tile.at[x], dst_ref=wy.at[y, z], send_sem=wz_s.at[s], recv_sem=wz_r.at[s],
            device_id=device(dz=s), device_id_type=MESH,
        )

    def fy_copy(t):
        dev = device(dy=t // 2, dc=t % 2)
        d = (dev["lon"] % 2) * 4 + dev["lev"]
        return pltpu.make_async_remote_copy(
            src_ref=f0.at[d], dst_ref=fy.at[c * 4 + y], send_sem=fy_s.at[t], recv_sem=fy_r.at[t],
            device_id=dev, device_id_type=MESH,
        )

    def wy_copy(t):
        return pltpu.make_async_remote_copy(
            src_ref=wy.at[y], dst_ref=wy.at[y], send_sem=wy_s.at[t], recv_sem=wy_r.at[t],
            device_id=device(dy=t), device_id_type=MESH,
        )

    def fz_copy(s):
        return pltpu.make_async_remote_copy(
            src_ref=fs.at[(z + s) % NZ], dst_ref=f_all.at[z], send_sem=fz_s.at[s], recv_sem=fz_r.at[s],
            device_id=device(dz=s), device_id_type=MESH,
        )

    def lanes(part):
        return pl.ds(pl.multiple_of(part * 128, 128), 128)

    def wx_copy(t):
        return pltpu.make_async_remote_copy(
            src_ref=regroup.at[pl.ds(1, 3)], dst_ref=w_all.at[:, :, c, :, lanes(x)],
            send_sem=wx_s.at[t], recv_sem=wx_r.at[t], device_id=device(dx=t), device_id_type=MESH,
        )

    def wc_copy(t):
        part = (x + NX - t) % NX
        return pltpu.make_async_remote_copy(
            src_ref=w_all.at[:, :, c, :, lanes(part)], dst_ref=w_all.at[:, :, c, :, lanes(part)],
            send_sem=wc_s.at[t], recv_sem=wc_r.at[t], device_id=device(dc=1), device_id_type=MESH,
        )

    def wc_land(t):
        part = (x + NX - t) % NX
        return pltpu.make_async_remote_copy(
            src_ref=w_all.at[:, :, 1 - c, :, lanes(part)], dst_ref=w_all.at[:, :, 1 - c, :, lanes(part)],
            send_sem=wc_s.at[t], recv_sem=wc_r.at[t], device_id=device(dc=1), device_id_type=MESH,
        )

    def qc_copy():
        return pltpu.make_async_remote_copy(
            src_ref=q_all.at[:, c], dst_ref=q_all.at[:, c],
            send_sem=wc_s.at[NX], recv_sem=wc_r.at[NX], device_id=device(dc=1), device_id_type=MESH,
        )

    def loop(lo, hi, act):
        def body(t, carry):
            act(t)
            return carry

        lax.fori_loop(lo, hi, body, 0)

    loop(0, NZ - 1, lambda t: wz_copy(far_first(t)).start())
    loop(1, 8, lambda t: fy_copy(t).start())
    wy[y, z] = tile[x]
    fy[c * 4 + y] = f0[c * 4 + y]

    loop(1, NZ, lambda s: wz_copy(s).wait_recv())
    loop(1, NY, lambda t: wy_copy(t).start())

    loop(1, 8, lambda t: fy_copy(t).wait_recv())
    slots = fy[:, :, ROW:ROWL].astype(F32).reshape(128, 128)
    at_row = iota((128, 128), 0)
    at_lane = iota((128, 128), 1)
    pick = (
        (slots == (at_lane % 16).astype(F32))
        & (at_row // 64 == at_lane // 32)
        & (at_row % 2 == (at_lane // 16) % 2)
    )
    pick = jnp.transpose(jnp.where(pick, 1.0, 0.0))[:64].astype(BF16)
    kept = jnp.dot(pick, fy[:, :, 0:ROW].reshape(128, ROW), preferred_element_type=F32)
    blank = jnp.zeros((16, 64), F32)
    for to in range(NZ):
        fs[to] = jnp.concatenate(
            [kept[16 * u : 16 * u + 16, to * IN : (to + 1) * IN] for u in range(4)] + [blank], axis=1
        ).astype(BF16)
    loop(0, NZ - 1, lambda t: fz_copy(far_first(t)).start())
    f_all[z] = fs[z]

    loop(1, NY, lambda t: wy_copy(t).wait_recv())

    def regroup_one(i, carry):
        rows = [wy[k, i].astype(F32) for k in range(NY)]
        for m in range(4):
            regroup[m, i] = jnp.concatenate([r[4 * m : 4 * m + 4] for r in rows], axis=0).astype(BF16)
        return carry

    lax.fori_loop(0, NZ, regroup_one, 0)
    loop(1, NX, lambda t: wx_copy(t).start())
    w_all[:, :, c, :, lanes(x)] = regroup[1:4]
    q_all[:, c] = regroup[0]
    wc_copy(0).start()
    qc_copy().start()

    def forward(t):
        wx_copy(t).wait_recv()
        wc_copy(t).start()

    loop(1, NX, forward)
    loop(1, NZ, lambda s: fz_copy(s).wait_recv())
    loop(0, NX, lambda t: wc_land(t).wait_recv())
    qc_copy().wait_recv()

    loop(1, NZ, lambda s: wz_copy(s).wait_send())
    loop(1, NZ, lambda s: fz_copy(s).wait_send())
    loop(1, 8, lambda t: fy_copy(t).wait_send())
    loop(1, NY, lambda t: wy_copy(t).wait_send())
    loop(1, NX, lambda t: wx_copy(t).wait_send())
    loop(0, NX, lambda t: wc_copy(t).wait_send())
    qc_copy().wait_send()


def exchange(fields, slot_level, latent, qkv, out_w):
    dma = pltpu.SemaphoreType.DMA
    vmem = pl.BlockSpec(memory_space=pltpu.VMEM)
    return pl.pallas_call(
        exchange_kernel,
        out_shape=(
            jax.ShapeDtypeStruct((3, NZ, NC, 16, D), BF16),
            jax.ShapeDtypeStruct((NZ, NC, 16, 128), BF16),
            jax.ShapeDtypeStruct((NZ, 16, 384), BF16),
        ),
        in_specs=[vmem, pl.BlockSpec(memory_space=pltpu.SMEM), vmem, vmem, vmem],
        out_specs=(vmem, vmem, vmem),
        scratch_shapes=[
            pltpu.VMEM((NX, 16, 128), BF16),
            pltpu.VMEM((NY, NZ, 16, 128), BF16),
            pltpu.VMEM((4, NZ, 16, 128), BF16),
            pltpu.VMEM((8, 16, ROWL), BF16),
            pltpu.VMEM((8, 16, ROWL), BF16),
            pltpu.VMEM((NZ, 16, 384), BF16),
            dma((NZ,)), dma((NZ,)),
            dma((NY,)), dma((NY,)),
            dma((NX,)), dma((NX,)),
            dma((NX + 1,)), dma((NX + 1,)),
            dma((8,)), dma((8,)),
            dma((NZ,)), dma((NZ,)),
        ],
        compiler_params=pltpu.CompilerParams(
            collective_id=0, has_side_effects=True, vmem_limit_bytes=32 * 1024 * 1024
        ),
        name="exchange",
    )(fields, slot_level, latent, qkv, out_w)


def compute_kernel(w, qt, f, embed_weight, level_encoding, out, shifted):
    scale = 1.0 / math.sqrt(D // HEADS)
    r = iota((LEVELS * 16, 256), 0)
    j = iota((LEVELS * 16, 256), 1)
    perm = jnp.where(j == (r % 16) * 16 + r // 16, 1.0, 0.0).astype(BF16)
    rows = jnp.dot(perm, f[...], preferred_element_type=F32).astype(BF16)
    shifted[...] = jnp.zeros_like(shifted)
    starts = (0, IN, 2 * IN - 128, 3 * IN - 128)
    for u in range(4):
        shifted[u, starts[u] : starts[u] + IN, :] = embed_weight[...]
    windows = ((0, 128), (0, 256), (128, 256), (128, 384))
    encoding = jnp.broadcast_to(
        level_encoding[...].astype(F32)[:, None, :], (LEVELS, 16, D)
    ).reshape(LEVELS * 16, D)

    fi = iota((D, 128), 0)
    li = iota((D, 128), 1)
    qv = qt[...].astype(F32)
    qblk = jnp.zeros((D, 128), F32)
    for a in range(LATENT):
        qblk = jnp.where(li == a * HEADS + fi // 32, qv[:, a : a + 1], qblk)
    qblk = qblk.astype(BF16)
    ki = iota((256, D), 0) % 128
    head = iota((256, D), 1) // 32
    spread = [jnp.where(ki == a * HEADS + head, 1.0, 0.0).astype(BF16) for a in range(LATENT)]

    mixed = [[] for _ in range(LATENT)]
    for u in range(4):
        lo, hi = windows[u]
        emb = (
            jnp.dot(rows[:, lo:hi], shifted[u, : hi - lo, :], preferred_element_type=F32) + encoding
        ).astype(BF16)
        keys = nt(emb, w[0]).astype(BF16)
        scores = (jnp.dot(keys, qblk, preferred_element_type=F32) * scale).reshape(LEVELS, 16, 128)
        highest = jnp.max(scores, axis=0, keepdims=True)
        expo = jnp.exp(scores - highest)
        weight = (expo / jnp.sum(expo, axis=0, keepdims=True)).reshape(LEVELS * 16, 128)
        top = weight.astype(BF16)
        low = (weight - top.astype(F32)).astype(BF16)
        both = jnp.concatenate([top, low], axis=1)
        values = nt(emb, w[1]).astype(BF16).astype(F32)
        for a in range(LATENT):
            wide = jnp.dot(both, spread[a], preferred_element_type=F32)
            mixed[a].append(jnp.sum((wide * values).reshape(LEVELS, 16, D), axis=0).astype(BF16))
    r = iota((64, 64), 0)
    j = iota((64, 64), 1)
    order = jnp.where(j == (r % 4) * 16 + r // 4, 1.0, 0.0).astype(BF16)
    for a in range(LATENT):
        block = jnp.dot(order, jnp.concatenate(mixed[a], axis=0), preferred_element_type=F32).astype(BF16)
        out[a] = nt(block, w[2]).astype(BF16)


def compute(w, qt, f, embed_weight, level_encoding):
    vmem = pl.BlockSpec(memory_space=pltpu.VMEM)
    return pl.pallas_call(
        compute_kernel,
        out_shape=jax.ShapeDtypeStruct((LATENT, 64, D), BF16),
        in_specs=[vmem] * 5,
        out_specs=vmem,
        scratch_shapes=[pltpu.VMEM((4, 256, D), BF16)],
        compiler_params=pltpu.CompilerParams(vmem_limit_bytes=32 * 1024 * 1024),
        cost_estimate=pl.CostEstimate(flops=2 * 10**9, bytes_accessed=3 * 10**6, transcendentals=10**5),
        name="attend",
    )(w, qt, f, embed_weight, level_encoding)


def on_device(fields, slot_level, embed_weight, level_encoding, latent_queries, qkv_weight, out_weight):
    w, q, f = exchange(fields, slot_level, latent_queries, qkv_weight, out_weight)
    out = compute(
        w.reshape(3, D, D), q.reshape(D, 128), f.reshape(NZ * 16, 384), embed_weight, level_encoding
    )
    return out.reshape(LATENT, 1, 64, D)


def solution(mesh):
    in_specs = (
        P("lev", "lon", "lat"),
        P("lev"),
        P(),
        P(),
        P(),
        P(None, ("lon", "lev"), None),
        P(("lon", "lev"), None),
    )
    out_specs = P(None, ("lat", "lon", "lev"), None, None)
    return jax.shard_map(
        on_device, mesh=mesh, in_specs=in_specs, out_specs=out_specs, check_vma=False
    )
```

time: 664 us -> 51.7 us (0.08)
  blocking collectives: 281 us -> 0 us
  waiting for transfers between devices: 190 us -> 0 us
  local copies, waits for them, and re-layouts: 126 us -> 5.28 us
  Pallas kernels: 0 us -> 46.1 us
  other arithmetic: 29.1 us -> 0 us
  between operations: 13.6 us -> 0.02 us
  starting transfers between devices: 13.3 us -> 0 us
  matrix products: 7.61 us -> 0 us
    all_gather x3 -> x0, blocking collectives: 281 us -> none  [the longest x1 261 us: on_device(): lax.all_gather(out_weight, ('lon', 'lev'), axis=0, tiled=True)]
    all_gather x2 -> x0, waiting for transfers between devices: 145 us -> none  [the longest x1 145 us: on_device(): weights = lax.all_gather(qkv_weight, ('lon', 'lev'), axis=1, tiled=True)]
    mul x26 -> x0, local copies, waits for them, and re-layouts: 96.8 us -> none  [the longest x16 73.6 us: rescale(): weighted.reshape(factor.shape + (-1,)) * factor[..., None]]
    pallas_call x0 -> x2, Pallas kernels: none -> 46.1 us  [the longest x1 41.2 us: exchange(): pl.pallas_call(exchange_kernel, out_shape=(jax.ShapeDtypeStruct((3, NZ, N...]
    all_to_all x1 -> x0, waiting for transfers between devices: 44.6 us -> none  [on_device(): lax.all_to_all(blocks, 'lon', split_axis=1, concat_axis=4, tiled=True)]
    add x8 -> x0, other arithmetic: 21 us -> none  [the longest x3 10.8 us: combine(): weighted = rescale(weighted_a, factor_a) + rescale(weighted_b, factor_b)]
    all_to_all x1 -> x0, starting transfers between devices: 13.3 us -> none  [on_device(): lax.all_to_all(blocks, 'lon', split_axis=1, concat_axis=4, tiled=True)]
    reshape x6 -> x0, local copies, waits for them, and re-layouts: 12.9 us -> none  [the longest x1 5.99 us: on_device(): weighted.reshape(grid_shape + (head_dim,))]
  transfers between devices with their start and end apart: 3 -> 0, of which waited for: 2 -> 0; matrix products, arithmetic and copies ran while one was open for 1% -> 0% of each run, Pallas kernels for 0% -> 0%
where the time goes in v1:
time: 51.7 us; the launch traced here: 51.4 us
  Pallas kernels  46.1 us (89%)
  local copies, waits for them, and re-layouts  5.28 us (10%)
    pallas_call x1, Pallas kernels, exchange(): pl.pallas_call(exchange_kernel, out_shape=(jax.ShapeDtypeStruct((3, NZ, N...  41.2 us
    unnamed x14, local copies, waits for them, and re-layouts  5.28 us
    pallas_call x1, Pallas kernels, compute(): pl.pallas_call(compute_kernel, out_shape=jax.ShapeDtypeStruct((LATENT, 64...  4.82 us

profile of v1, /device:TPU:1, one launch (start us, length us, event | category | flops | bytes accessed | tf_op | source)
XLA Modules:
  0.0 51.4 jit_solution(2945505166415546775)
XLA Ops:
  0.0 0.0 copy-start
  0.0 0.9 %copy-done = bf16[6,2,10240]{2,1,0:T(2,128)(2,1)S(1)} copy-done((bf16[6,2,10240]{2,1,0:T(2,128)(2,1)S(1)}, bf16[6,2,10240]{2,1,0:T(2,128)(2,1)}, u32[]{:S(2)}) %copy-start) | copy-done | bytes 245784
  0.9 0.0 copy-start.1
  0.9 0.7 %copy-done.1 = bf16[3,4,512]{2,1,0:T(4,128)(2,1)S(1)} copy-done((bf16[3,4,512]{2,1,0:T(4,128)(2,1)S(1)}, bf16[3,4,512]{2,1,0:T(4,128)(2,1)}, u32[]{:S(2)}) %copy-start.1) | copy-done | bytes 12312
  1.7 0.0 copy-start.2
  1.7 0.7 %copy-done.2 = bf16[3,512]{1,0:T(4,128)(2,1)S(1)} copy-done((bf16[3,512]{1,0:T(4,128)(2,1)S(1)}, bf16[3,512]{1,0:T(4,128)(2,1)}, u32[]{:S(2)}) %copy-start.2) | copy-done | bytes 3096
  2.3 0.0 copy-start.3
  2.3 0.7 %copy-done.3 = bf16[4,512]{1,0:T(4,128)(2,1)S(1)} copy-done((bf16[4,512]{1,0:T(4,128)(2,1)S(1)}, bf16[4,512]{1,0:T(4,128)(2,1)}, u32[]{:S(2)}) %copy-start.3) | copy-done | bytes 4120
  3.0 0.0 copy-start.4
  3.0 0.7 %copy-done.4 = s32[6]{0:T(128)S(1)} copy-done((s32[6]{0:T(128)S(1)}, s32[6]{0:T(128)}, u32[]{:S(2)}) %copy-start.4) | copy-done | bytes 48
  3.7 41.2 %exchange.1 = (bf16[3,16,2,16,512]{4,3,2,1,0:T(8,128)(2,1)S(1)}, bf16[16,2,16,128]{3,2,1,0:T(8,128)(2,1)S(1)}, bf16[16,16,384]{2,1,0:T(8,128)(2,1)S(1)}) custom-call(bf16[6,2,10240]{2,1,0:T(2,128)(2,1)S(1)} %copy-done, s32[6]{0:T(128)S(1)} %copy-done.4, bf16[3,512]{1,0:T(4,128)(2,1)S(1)} %copy-done.2, bf16[3,4,512]{2,1,0:T(4,128)(2,1)S(1)} %copy-done.1, ...), custom_call_target="tpu_custom_call" | custom-call | tf_op jit(solution)/shard_map/exchange/pallas_call | solution.py:235
  44.9 0.0 copy-start.5
  44.9 0.9 %copy-done.5 = bf16[80,512]{1,0:T(8,128)(2,1)S(1)} copy-done((bf16[80,512]{1,0:T(8,128)(2,1)S(1)}, bf16[80,512]{1,0:T(8,128)(2,1)}, u32[]{:S(2)}) %copy-start.5) | copy-done | bytes 81944
  45.8 0.0 copy-start.6
  45.8 0.7 %copy-done.6 = bf16[14,512]{1,0:T(8,128)(2,1)S(1)} copy-done((bf16[14,512]{1,0:T(8,128)(2,1)S(1)}, bf16[14,512]{1,0:T(8,128)(2,1)}, u32[]{:S(2)}) %copy-start.6) | copy-done | bytes 14360
  46.5 4.8 %attend.1 = bf16[3,64,512]{2,1,0:T(8,128)(2,1)} custom-call(bf16[3,512,512]{2,1,0:T(8,128)(2,1)S(1)} %bitcast.6, bf16[512,128]{1,0:T(8,128)(2,1)S(1)} %bitcast.8, bf16[256,384]{1,0:T(8,128)(2,1)S(1)} %bitcast.7, bf16[80,512]{1,0:T(8,128)(2,1)S(1)} %copy-done.5, bf16[14,512]{1,0:T(8,128)(2,1)S(1)} %copy-done.6), custom_call_target="tpu_custom_call" | custom-call | flops 2000000000 | bytes 3000000 | tf_op jit(solution)/shard_map/attend/pallas_call | solution.py:319
Async XLA Ops:
  0.0 0.9 %copy-start = (bf16[6,2,10240]{2,1,0:T(2,128)(2,1)S(1)}, bf16[6,2,10240]{2,1,0:T(2,128)(2,1)}, u32[]{:S(2)}) copy-start(bf16[6,2,10240]{2,1,0:T(2,128)(2,1)} %fields.1) | copy-start | bytes 737284
  0.9 0.7 %copy-start.1 = (bf16[3,4,512]{2,1,0:T(4,128)(2,1)S(1)}, bf16[3,4,512]{2,1,0:T(4,128)(2,1)}, u32[]{:S(2)}) copy-start(bf16[3,4,512]{2,1,0:T(4,128)(2,1)} %qkv.1) | copy-start | bytes 36868
  1.7 0.7 %copy-start.2 = (bf16[3,512]{1,0:T(4,128)(2,1)S(1)}, bf16[3,512]{1,0:T(4,128)(2,1)}, u32[]{:S(2)}) copy-start(bf16[3,512]{1,0:T(4,128)(2,1)} %latent.1) | copy-start | bytes 9220
  2.3 0.7 %copy-start.3 = (bf16[4,512]{1,0:T(4,128)(2,1)S(1)}, bf16[4,512]{1,0:T(4,128)(2,1)}, u32[]{:S(2)}) copy-start(bf16[4,512]{1,0:T(4,128)(2,1)} %out_w.1) | copy-start | bytes 12292
  3.0 0.7 %copy-start.4 = (s32[6]{0:T(128)S(1)}, s32[6]{0:T(128)}, u32[]{:S(2)}) copy-start(s32[6]{0:T(128)} %slot_level.1) | copy-start | bytes 76
  44.9 0.9 %copy-start.5 = (bf16[80,512]{1,0:T(8,128)(2,1)S(1)}, bf16[80,512]{1,0:T(8,128)(2,1)}, u32[]{:S(2)}) copy-start(bf16[80,512]{1,0:T(8,128)(2,1)} %embed_weight.1) | copy-start | bytes 245764
  45.8 0.7 %copy-start.6 = (bf16[14,512]{1,0:T(8,128)(2,1)S(1)}, bf16[14,512]{1,0:T(8,128)(2,1)}, u32[]{:S(2)}) copy-start(bf16[14,512]{1,0:T(8,128)(2,1)} %level_encoding.1) | copy-start | bytes 43012

commit v2 on v0

v2 whole, which is shorter than its diff:
```python
import math

import jax
import jax.numpy as jnp
from jax import lax
from jax.experimental import pallas as pl
from jax.experimental.pallas import tpu as pltpu
from jax.sharding import PartitionSpec as P

MESH = pl.DeviceIdType.MESH
F32 = jnp.float32
BF16 = jnp.bfloat16
NZ, NY, NX, NC = 16, 4, 4, 2
NXY = NX * NY
IN = 80
D = 512
LEVELS = 14
HEADS = 16
LATENT = 3
UNITS = 8 * IN
ROWS = LEVELS * 16
VMEM_LIMIT = 60 * 1024 * 1024


def iota(shape, dim):
    return lax.broadcasted_iota(jnp.int32, shape, dim)


def one_hot(mask):
    return jnp.where(mask, 1.0, 0.0).astype(BF16)


def dot(a, b):
    return jnp.dot(a, b, preferred_element_type=F32)


def nt(a, b):
    return lax.dot_general(a, b, (((1,), (1,)), ((), ())), preferred_element_type=F32)


def offset(k):
    return (NZ + (k % 2) * ((k + 1) // 2) - (1 - k % 2) * (k // 2)) % NZ


def loop(lo, hi, act):
    def body(t, carry):
        act(t)
        return carry

    lax.fori_loop(lo, hi, body, 0)


def kernel(
    fields_h, slot_h, latent_h, qkv_h, out_w_h, embed_h, encode_h,
    out,
    fields, slot_level, latent, qkv, out_w, embed, encode,
    tile, wz, pack, w_all, q_all, f0a, f0b, fya, fyb, kept, fs, fz,
    shifted, emb, qblk, spread, natural, mixed,
    in_s, wz_s, wz_r, wp_s, wp_r, wq_s, wq_r, wc_s, wc_r, fy_s, fy_r, fz_s, fz_r,
):
    x = lax.axis_index("lat")
    lon = lax.axis_index("lon")
    y = lax.axis_index("lev")
    z = lon // 2
    c = lon % 2

    def device(dx=0, dy=0, dz=0, dc=0):
        return {
            "lat": (x + dx) % NX,
            "lon": ((z + dz) % NZ) * 2 + (c + dc) % 2,
            "lev": (y + dy) % NY,
        }

    barrier = pltpu.get_barrier_semaphore()

    def greet(dev):
        pl.semaphore_signal(barrier, inc=1, device_id=dev, device_id_type=MESH)

    loop(1, NZ, lambda k: greet(device(dz=offset(NZ - k))))
    loop(1, NXY, lambda t: greet(device(dx=t // NY, dy=t % NY)))
    loop(0, NY, lambda t: greet(device(dy=t, dc=1)))

    loads = [
        pltpu.make_async_copy(src, dst, in_s.at[i])
        for i, (src, dst) in enumerate(
            (
                (qkv_h, qkv), (out_w_h, out_w), (latent_h, latent), (slot_h, slot_level),
                (fields_h, fields), (embed_h, embed), (encode_h, encode),
            )
        )
    ]
    for load in loads:
        load.start()
    for load in loads[:3]:
        load.wait()

    wq = qkv[0].astype(F32)
    lat = latent[...].astype(F32)
    lane = iota((4, 128), 1)
    q = jnp.zeros((4, 128), F32)
    for a in range(LATENT):
        col = jnp.sum(wq * lat[a : a + 1, :], axis=1, keepdims=True)
        q = jnp.where(lane == a, col, q)
    for part in range(NX):
        cut_at = slice(part * 128, part * 128 + 128)
        tile[part] = jnp.concatenate(
            [q, qkv[1, :, cut_at].astype(F32), qkv[2, :, cut_at].astype(F32), out_w[:, cut_at].astype(F32)],
            axis=0,
        ).astype(BF16)
    wz[0] = tile[x]

    for load in loads[3:5]:
        load.wait()
    for half, f0 in ((1, f0a), (0, f0b)):
        blocks = []
        for e in range(8):
            to = (z + NZ - offset(8 * half + e)) % NZ
            at = pl.ds(pl.multiple_of(to * UNITS, 128), UNITS)
            rows = [fields[s, :, at].astype(F32) for s in range(6)]
            blocks.append(jnp.concatenate(rows + [jnp.zeros((4, UNITS), F32)], axis=0))
        for d in range(8):
            f0[d, :, 0:UNITS] = jnp.concatenate(
                [blocks[e][:, d * IN : (d + 1) * IN] for e in range(8)], axis=1
            ).astype(BF16)
    slot_of_row = iota((16, 128), 0) // 2
    levels = jnp.full((16, 128), -1.0, F32)
    for s in range(6):
        levels = jnp.where(slot_of_row == s, slot_level[s].astype(F32), levels)
    for d in range(8):
        f0a[d, :, UNITS:] = levels.astype(BF16)
    fya[c * 4 + y] = f0a[c * 4 + y]
    fyb[c * 4 + y] = f0b[c * 4 + y]

    def remote(src, dst, send, recv, dev):
        return pltpu.make_async_remote_copy(
            src_ref=src, dst_ref=dst, send_sem=send, recv_sem=recv, device_id=dev, device_id_type=MESH
        )

    def wz_copy(k):
        return remote(tile.at[x], wz.at[k], wz_s.at[k], wz_r.at[k], device(dz=NZ - offset(k)))

    def fy_copy(t, half):
        dev = device(dy=t // 2, dc=t % 2)
        d = (dev["lon"] % 2) * 4 + dev["lev"]
        f0, fy = ((f0b, fyb), (f0a, fya))[half]
        return remote(f0.at[d], fy.at[c * 4 + y], fy_s.at[half, t], fy_r.at[half, t], dev)

    def fz_copy(k):
        return remote(fs.at[k], fz.at[z], fz_s.at[k], fz_r.at[k], device(dz=NZ - offset(k)))

    lanes = pl.ds(pl.multiple_of(x * 128, 128), 128)

    def wp_copy(t, i):
        what, which = ((slice(0, 2), slice(0, 2)), (slice(0, 2), slice(2, 4)), (slice(2, 3), slice(0, 4)))[i]
        return remote(
            pack.at[what, which], w_all.at[what, c, y, which, :, lanes], wp_s.at[i, t], wp_r.at[i, t],
            device(dx=t // NY, dy=t % NY),
        )

    def wq_copy(t):
        return remote(pack.at[3], q_all.at[c, y], wq_s.at[t], wq_r.at[t], device(dy=t))

    def wc_copy(m, side):
        ref = q_all.at[side] if m == 3 else w_all.at[m, side]
        return remote(ref, ref, wc_s.at[m], wc_r.at[m], device(dc=1))

    def regroup(i):
        rows = [wz[4 * i + j].astype(F32) for j in range(4)]
        for m, at in ((3, 0), (0, 4), (1, 8), (2, 12)):
            block = jnp.concatenate([r[at : at + 4] for r in rows], axis=0).astype(BF16)
            pack[m, i] = block
            if m == 3:
                q_all[c, y, i] = block
            else:
                w_all[m, c, y, i, :, lanes] = block

    pl.semaphore_wait(barrier, NZ - 1 + NXY - 1 + NY)
    loop(1, NZ, lambda k: wz_copy(NZ - k).start())
    loop(1, 8, lambda t: fy_copy(t, 1).start())
    loop(1, 8, lambda t: fy_copy(t, 0).start())
    for load in loads[5:]:
        load.wait()
    shifted[...] = jnp.zeros_like(shifted)
    starts = (0, IN, 2 * IN - 128, 3 * IN - 128)
    for u in range(4):
        shifted[u, starts[u] : starts[u] + IN, :] = embed[...]

    def head_of(g):
        k = (g // 4) % NZ
        return (z + jnp.where(k % 2 == 1, (k + 1) // 2, NZ - k // 2)) % NZ

    g = iota((D, D), 0)
    natural[...] = one_hot(iota((D, D), 1) == head_of(g) * 32 + (g // 256) * 16 + (g // 64) % 4 * 4 + g % 4)
    ki = iota((256, D), 0) % 128
    head = head_of(iota((256, D), 1))
    for a in range(LATENT):
        spread[a] = one_hot(ki == a * HEADS + head)

    loop(1, 8, lambda t: fy_copy(t, 1).wait_recv())
    slots = fya[:, :, UNITS:].astype(F32).reshape(128, 128)
    at_row = iota((128, 128), 0)
    at_lane = iota((128, 128), 1)
    pick = (
        (slots == (at_lane % 16).astype(F32))
        & (at_row // 64 == at_lane // 32)
        & (at_row % 2 == (at_lane // 16) % 2)
    )
    pick = jnp.transpose(jnp.where(pick, 1.0, 0.0))[:64].astype(BF16)
    blank = jnp.zeros((16, 64), F32)

    def keep(half, fy):
        kept[...] = dot(pick, fy[:, :, 0:UNITS].reshape(128, UNITS))
        for e in range(8):
            fs[8 * half + e] = jnp.concatenate(
                [kept[16 * u : 16 * u + 16, e * IN : (e + 1) * IN] for u in range(4)] + [blank], axis=1
            ).astype(BF16)

    keep(1, fya)
    loop(0, 8, lambda k: fz_copy(NZ - 1 - k).start())
    loop(1, 8, lambda t: fy_copy(t, 0).wait_recv())
    keep(0, fyb)
    loop(1, 8, lambda k: fz_copy(8 - k).start())
    fz[z] = fs[0]

    loop(1, 8, lambda k: wz_copy(k).wait_recv())
    regroup(0)
    regroup(1)
    loop(1, NXY, lambda t: wp_copy(t, 0).start())
    loop(8, NZ, lambda k: wz_copy(k).wait_recv())
    regroup(2)
    regroup(3)
    loop(1, NXY, lambda t: wp_copy(t, 1).start())
    loop(1, NY, lambda t: wq_copy(t).start())
    loop(1, NXY, lambda t: wp_copy(t, 2).start())

    loop(1, NZ, lambda k: fz_copy(k).wait_recv())
    r = iota((ROWS, 256), 0)
    j = iota((ROWS, 256), 1)
    rows = dot(one_hot(j == (r % 16) * 16 + r // 16), fz[...].reshape(256, 384)).astype(BF16)
    encoding = jnp.broadcast_to(encode[...].astype(F32)[:, None, :], (LEVELS, 16, D)).reshape(ROWS, D)
    for u, (lo, hi) in enumerate(((0, 128), (0, 256), (128, 256), (128, 384))):
        emb[u] = (dot(rows[:, lo:hi], shifted[u, : hi - lo, :]) + encoding).astype(BF16)

    loop(1, NY, lambda t: wq_copy(t).wait_recv())
    wc_copy(3, c).start()
    loop(1, NXY, lambda t: wp_copy(t, 0).wait_recv())
    loop(1, NXY, lambda t: wp_copy(t, 1).wait_recv())
    wc_copy(0, c).start()
    wc_copy(1, c).start()
    wc_copy(3, 1 - c).wait_recv()
    wc_copy(0, 1 - c).wait_recv()
    wc_copy(1, 1 - c).wait_recv()

    scale = 1.0 / math.sqrt(D // HEADS)
    g = iota((D, 128), 0)
    at_lane = iota((D, 128), 1)
    qv = q_all[...].astype(F32).reshape(D, 128)
    found = jnp.zeros((D, 128), F32)
    for a in range(LATENT):
        found = jnp.where(at_lane == a * HEADS + head_of(g), qv[:, a : a + 1], found)
    qblk[...] = found.astype(BF16)
    k_w = w_all.at[0]
    v_w = w_all.at[1]
    for u in range(4):
        keys = nt(emb[u], k_w[...].reshape(D, D)).astype(BF16)
        scores = (dot(keys, qblk[...]) * scale).reshape(LEVELS, 16, 128)
        highest = jnp.max(scores, axis=0, keepdims=True)
        expo = jnp.exp(scores - highest)
        weight = (expo / jnp.sum(expo, axis=0, keepdims=True)).reshape(ROWS, 128)
        top = weight.astype(BF16)
        low = (weight - top.astype(F32)).astype(BF16)
        both = jnp.concatenate([top, low], axis=1)
        values = nt(emb[u], v_w[...].reshape(D, D)).astype(BF16).astype(F32)
        for a in range(LATENT):
            wide = dot(both, spread[a])
            mixed[a, 16 * u : 16 * u + 16] = jnp.sum(
                (wide * values).reshape(LEVELS, 16, D), axis=0
            ).astype(BF16)
    loop(1, NXY, lambda t: wp_copy(t, 2).wait_recv())
    wc_copy(2, c).start()
    r = iota((64, 64), 0)
    j = iota((64, 64), 1)
    order = one_hot(j == (r % 4) * 16 + r // 4)
    block = jnp.concatenate([dot(order, mixed[a]).astype(BF16) for a in range(LATENT)], axis=0)
    block = dot(block, natural[...]).astype(BF16)
    wc_copy(2, 1 - c).wait_recv()
    block = nt(block, w_all[2].reshape(D, D)).astype(BF16)
    out[...] = dot(block, natural[...]).astype(BF16).reshape(LATENT, 64, D)

    loop(1, NZ, lambda k: wz_copy(k).wait_send())
    loop(1, NZ, lambda k: fz_copy(k).wait_send())
    for half in range(2):
        loop(1, 8, lambda t: fy_copy(t, half).wait_send())
    for i in range(3):
        loop(1, NXY, lambda t: wp_copy(t, i).wait_send())
    loop(1, NY, lambda t: wq_copy(t).wait_send())
    for m in range(4):
        wc_copy(m, c).wait_send()


def encode_patches(*operands):
    dma = pltpu.SemaphoreType.DMA
    vmem = pltpu.VMEM
    fields, slot_level, latent, qkv, out_w, embed, encode = operands
    return pl.pallas_call(
        kernel,
        out_shape=jax.ShapeDtypeStruct((LATENT, 64, D), BF16),
        in_specs=[pl.BlockSpec(memory_space=pltpu.HBM)] * 7,
        out_specs=pl.BlockSpec(memory_space=pltpu.VMEM),
        scratch_shapes=[
            vmem(fields.shape, BF16),
            pltpu.SMEM(slot_level.shape, jnp.int32),
            vmem(latent.shape, BF16),
            vmem(qkv.shape, BF16),
            vmem(out_w.shape, BF16),
            vmem(embed.shape, BF16),
            vmem(encode.shape, BF16),
            vmem((NX, 16, 128), BF16),
            vmem((NZ, 16, 128), BF16),
            vmem((4, 4, 16, 128), BF16),
            vmem((3, NC, NY, 4, 16, D), BF16),
            vmem((NC, NY, 4, 16, 128), BF16),
            vmem((8, 16, UNITS + 128), BF16),
            vmem((8, 16, UNITS), BF16),
            vmem((8, 16, UNITS + 128), BF16),
            vmem((8, 16, UNITS), BF16),
            vmem((64, UNITS), F32),
            vmem((NZ, 16, 384), BF16),
            vmem((NZ, 16, 384), BF16),
            vmem((4, 256, D), BF16),
            vmem((4, ROWS, D), BF16),
            vmem((D, 128), BF16),
            vmem((LATENT, 256, D), BF16),
            vmem((D, D), BF16),
            vmem((LATENT, 64, D), BF16),
            dma((7,)),
            dma((NZ,)), dma((NZ,)),
            dma((3, NXY)), dma((3, NXY)),
            dma((NY,)), dma((NY,)),
            dma((4,)), dma((4,)),
            dma((2, 8)), dma((2, 8)),
            dma((NZ,)), dma((NZ,)),
        ],
        compiler_params=pltpu.CompilerParams(
            collective_id=0, has_side_effects=True, vmem_limit_bytes=VMEM_LIMIT
        ),
        cost_estimate=pl.CostEstimate(flops=3 * 10**9, bytes_accessed=10**6, transcendentals=10**5),
        name="encode_patches",
    )(*operands)


def on_device(fields, slot_level, embed_weight, level_encoding, latent_queries, qkv_weight, out_weight):
    out = encode_patches(
        fields, slot_level, latent_queries, qkv_weight, out_weight, embed_weight, level_encoding
    )
    return out.reshape(LATENT, 1, 64, D)


def solution(mesh):
    in_specs = (
        P("lev", "lon", "lat"),
        P("lev"),
        P(),
        P(),
        P(),
        P(None, ("lon", "lev"), None),
        P(("lon", "lev"), None),
    )
    out_specs = P(None, ("lat", "lon", "lev"), None, None)
    return jax.shard_map(
        on_device, mesh=mesh, in_specs=in_specs, out_specs=out_specs, check_vma=False
    )
```

time: 664 us -> 45.2 us (0.07)
  blocking collectives: 281 us -> 0 us
  waiting for transfers between devices: 190 us -> 0 us
  local copies, waits for them, and re-layouts: 126 us -> 1.62 us
  Pallas kernels: 0 us -> 43.1 us
  other arithmetic: 29.1 us -> 0 us
  between operations: 13.6 us -> 0.01 us
  starting transfers between devices: 13.3 us -> 0 us
  matrix products: 7.61 us -> 0 us
    all_gather x3 -> x0, blocking collectives: 281 us -> none  [the longest x1 261 us: on_device(): lax.all_gather(out_weight, ('lon', 'lev'), axis=0, tiled=True)]
    all_gather x2 -> x0, waiting for transfers between devices: 145 us -> none  [the longest x1 145 us: on_device(): weights = lax.all_gather(qkv_weight, ('lon', 'lev'), axis=1, tiled=True)]
    mul x26 -> x0, local copies, waits for them, and re-layouts: 96.8 us -> none  [the longest x16 73.6 us: rescale(): weighted.reshape(factor.shape + (-1,)) * factor[..., None]]
    all_to_all x1 -> x0, waiting for transfers between devices: 44.6 us -> none  [on_device(): lax.all_to_all(blocks, 'lon', split_axis=1, concat_axis=4, tiled=True)]
    pallas_call x0 -> x1, Pallas kernels: none -> 43.1 us  [encode_patches(): pl.pallas_call(kernel, out_shape=jax.ShapeDtypeStruct((LATENT, 64, D), BF...]
    add x8 -> x0, other arithmetic: 21 us -> none  [the longest x3 10.8 us: combine(): weighted = rescale(weighted_a, factor_a) + rescale(weighted_b, factor_b)]
    all_to_all x1 -> x0, starting transfers between devices: 13.3 us -> none  [on_device(): lax.all_to_all(blocks, 'lon', split_axis=1, concat_axis=4, tiled=True)]
    reshape x6 -> x0, local copies, waits for them, and re-layouts: 12.9 us -> none  [the longest x1 5.99 us: on_device(): weighted.reshape(grid_shape + (head_dim,))]
  transfers between devices with their start and end apart: 3 -> 0, of which waited for: 2 -> 0; matrix products, arithmetic and copies ran while one was open for 1% -> 0% of each run, Pallas kernels for 0% -> 0%
where the time goes in v2:
time: 45.2 us; the launch traced here: 44.8 us
  Pallas kernels  43.1 us (95%)
  local copies, waits for them, and re-layouts  1.62 us (4%)
    pallas_call x1, Pallas kernels, encode_patches(): pl.pallas_call(kernel, out_shape=jax.ShapeDtypeStruct((LATENT, 64, D), BF...  43.1 us
    unnamed x1, local copies, waits for them, and re-layouts  1.62 us

profile of v2, /device:TPU:1, one launch (start us, length us, event | category | flops | bytes accessed | tf_op | source)
XLA Modules:
  0.0 44.8 jit_solution(8715957882883485645)
XLA Ops:
  0.0 43.1 %encode_patches.1 = bf16[3,64,512]{2,1,0:T(8,128)(2,1)} custom-call(bf16[6,2,10240]{2,1,0:T(2,128)(2,1)} %fields_h.1, s32[6]{0:T(128)} %slot_h.1, bf16[3,512]{1,0:T(4,128)(2,1)} %latent_h.1, bf16[3,4,512]{2,1,0:T(4,128)(2,1)} %qkv_h.1, bf16[4,512]{1,0:T(4,128)(2,1)} %out_w_h.1, bf16[80,512]{1,0:T(8,128)(2,1)} %embed_h.1, bf16[14,512]{1,0:T(8,128)(2,1)} %encode_h.1), custom_call_target="tpu_custom_call" | custom-call | flops 3000000000 | bytes 1000000 | tf_op jit(solution)/shard_map/encode_patches/pallas_call | solution.py:305
  43.1 1.6 %copy.10 = bf16[3,1,64,512]{3,2,1,0:T(8,128)(2,1)} copy(bf16[3,1,64,512]{3,2,1,0:T(8,128)(2,1)} %bitcast.3) | data formatting | bytes 393216

commit v3 on v2

v3 whole, which is shorter than its diff:
```python
import math

import jax
import jax.numpy as jnp
from jax import lax
from jax.experimental import pallas as pl
from jax.experimental.pallas import tpu as pltpu
from jax.sharding import PartitionSpec as P

MESH = pl.DeviceIdType.MESH
F32 = jnp.float32
BF16 = jnp.bfloat16
NZ, NY, NX, NC = 16, 4, 4, 2
IN = 80
D = 512
LEVELS = 14
HEADS = 16
LATENT = 3
UNITS = 8 * IN
ROWS = LEVELS * 16
VMEM_LIMIT = 40 * 1024 * 1024


def iota(shape, dim):
    return lax.broadcasted_iota(jnp.int32, shape, dim)


def one_hot(mask):
    return jnp.where(mask, 1.0, 0.0).astype(BF16)


def dot(a, b):
    return jnp.dot(a, b, preferred_element_type=F32)


def nt(a, b):
    return lax.dot_general(a, b, (((1,), (1,)), ((), ())), preferred_element_type=F32)


def offset(k):
    return (NZ + (k % 2) * ((k + 1) // 2) - (1 - k % 2) * (k // 2)) % NZ


def loop(lo, hi, act):
    def body(t, carry):
        act(t)
        return carry

    lax.fori_loop(lo, hi, body, 0)


def kernel(
    fields_h, slot_h, latent_h, qkv_h, out_w_h, embed_h, encode_h,
    out,
    fields, slot_level, latent, qkv, out_w, embed, encode,
    tile, wz, pack, w_kv, w_o, q_all, f0, fy, whole, kept, fs, fz,
    shifted, emb, spread, natural_t, mixed,
    in_s, wz_s, wz_r, wp_s, wp_r, wy_s, wy_r, wx_s, wx_r, wc_s, wc_r, fy_s, fy_r, fz_s, fz_r,
):
    x = lax.axis_index("lat")
    lon = lax.axis_index("lon")
    y = lax.axis_index("lev")
    z = lon // 2
    c = lon % 2

    def device(dx=0, dy=0, dz=0, dc=0):
        return {
            "lat": (x + dx) % NX,
            "lon": ((z + dz) % NZ) * 2 + (c + dc) % 2,
            "lev": (y + dy) % NY,
        }

    barrier = pltpu.get_barrier_semaphore()

    def greet(dev):
        pl.semaphore_signal(barrier, inc=1, device_id=dev, device_id_type=MESH)

    loop(1, NZ, lambda k: greet(device(dz=offset(NZ - k))))
    loop(1, NX, lambda t: greet(device(dx=t)))
    loop(1, 8, lambda t: greet(device(dy=t // 2, dc=t % 2)))

    loads = [
        pltpu.make_async_copy(src, dst, in_s.at[i])
        for i, (src, dst) in enumerate(
            (
                (qkv_h, qkv), (out_w_h, out_w), (latent_h, latent), (slot_h, slot_level),
                (fields_h, fields), (embed_h, embed), (encode_h, encode),
            )
        )
    ]
    for load in loads:
        load.start()
    for load in loads[:3]:
        load.wait()

    wq = qkv[0].astype(F32)
    lat = latent[...].astype(F32)
    lane = iota((4, 128), 1)
    q = jnp.zeros((4, 128), F32)
    for a in range(LATENT):
        col = jnp.sum(wq * lat[a : a + 1, :], axis=1, keepdims=True)
        q = jnp.where(lane == a, col, q)
    for part in range(NX):
        cut_at = slice(part * 128, part * 128 + 128)
        tile[part] = jnp.concatenate(
            [q, qkv[1, :, cut_at].astype(F32), qkv[2, :, cut_at].astype(F32), out_w[:, cut_at].astype(F32)],
            axis=0,
        ).astype(BF16)
    wz[0] = tile[x]

    for load in loads[3:5]:
        load.wait()
    at_row = iota((4, 128), 0)
    slot_of_lane = iota((4, 128), 1) // 2
    levels = jnp.full((4, 128), -1.0, F32)
    for s in range(6):
        levels = jnp.where(slot_of_lane == s, slot_level[s].astype(F32), levels)
    for half in (1, 0):
        blocks = []
        for e in range(8):
            to = (z + NZ - offset(8 * half + e)) % NZ
            at = pl.ds(pl.multiple_of(to * UNITS, 128), UNITS)
            blocks.append(jnp.concatenate([fields[s, :, at].astype(F32) for s in range(6)], axis=0))
        for d in range(8):
            units = jnp.concatenate([blocks[e][:, d * IN : (d + 1) * IN] for e in range(8)], axis=1)
            last = units[:, 512:]
            spare = jnp.concatenate([last[0:4], last[4:8], last[8:12], levels], axis=1)
            f0[half, d] = jnp.concatenate([units[:, :512], spare], axis=0).astype(BF16)
    for half in range(2):
        fy[half, c * 4 + y] = f0[half, c * 4 + y]

    def remote(src, dst, send, recv, dev):
        return pltpu.make_async_remote_copy(
            src_ref=src, dst_ref=dst, send_sem=send, recv_sem=recv, device_id=dev, device_id_type=MESH
        )

    def wz_copy(k):
        return remote(tile.at[x], wz.at[k], wz_s.at[k], wz_r.at[k], device(dz=NZ - offset(k)))

    def fy_copy(t, half):
        dev = device(dy=t // 2, dc=t % 2)
        d = (dev["lon"] % 2) * 4 + dev["lev"]
        return remote(f0.at[half, d], fy.at[half, c * 4 + y], fy_s.at[half, t], fy_r.at[half, t], dev)

    def fz_copy(k):
        return remote(fs.at[k], fz.at[z], fz_s.at[k], fz_r.at[k], device(dz=NZ - offset(k)))

    lanes = pl.ds(pl.multiple_of(x * 128, 128), 128)

    def near_y(t):
        return remote(
            pack.at[0, pl.ds(0, 2)], w_kv.at[0, :, c, y, :, :, lanes], wp_s.at[0, t], wp_r.at[0, t], device(dy=t)
        )

    def near_x(t):
        ref = w_kv.at[0, :, c, :, :, :, lanes]
        return remote(ref, ref, wp_s.at[1, t], wp_r.at[1, t], device(dx=t))

    def far_x(t):
        return remote(
            pack.at[1, pl.ds(0, 2)], w_kv.at[1, :, c, y, :, :, lanes], wp_s.at[2, t], wp_r.at[2, t], device(dx=t)
        )

    def far_y(t):
        ref = w_kv.at[1, :, c, y]
        return remote(ref, ref, wp_s.at[3, t], wp_r.at[3, t], device(dy=t))

    def wq_copy(t):
        return remote(pack.at[:, 3], q_all.at[:, c, y], wy_s.at[0, t], wy_r.at[0, t], device(dy=t))

    def wy_copy(t):
        return remote(pack.at[:, 2], w_o.at[:, c, y, :, :, lanes], wy_s.at[1, t], wy_r.at[1, t], device(dy=t))

    def wx_copy(t):
        ref = w_o.at[:, c, :, :, :, lanes]
        return remote(ref, ref, wx_s.at[t], wx_r.at[t], device(dx=t))

    def wc_copy(i, side):
        ref = (w_kv.at[0, :, side], w_kv.at[1, :, side], w_o.at[:, side], q_all.at[:, side])[i]
        return remote(ref, ref, wc_s.at[i], wc_r.at[i], device(dc=1))

    def regroup(half):
        for i in range(2):
            rows = [wz[8 * half + 4 * i + j].astype(F32) for j in range(4)]
            for m, at in enumerate((4, 8, 12, 0)):
                block = jnp.concatenate([r[at : at + 4] for r in rows], axis=0).astype(BF16)
                pack[half, m, i] = block
                if m == 3:
                    q_all[half, c, y, i] = block
                elif m == 2:
                    w_o[half, c, y, i, :, lanes] = block
                else:
                    w_kv[half, m, c, y, i, :, lanes] = block

    pl.semaphore_wait(barrier, NZ - 1 + NX - 1 + 7)
    loop(1, NZ, lambda k: wz_copy(NZ - k).start())
    loop(1, 8, lambda t: fy_copy(t, 1).start())
    for load in loads[5:]:
        load.wait()
    shifted[...] = jnp.zeros_like(shifted)
    starts = (0, IN, 2 * IN - 128, 3 * IN - 128)
    for u in range(4):
        shifted[u, starts[u] : starts[u] + IN, :] = embed[...]

    def head_of(g):
        k = ((g >> 8) << 3) | ((g >> 2) & 7)
        return (z + jnp.where((k & 1) == 1, (k + 1) >> 1, NZ - (k >> 1))) & (NZ - 1)

    g = iota((D, 128), 0)
    place = (head_of(g) * 32 + ((g >> 7) & 1) * 16 + ((g >> 5) & 3) * 4 + (g & 3))[:, :1]
    natural_t[...] = one_hot(iota((D, D), 1) == place)
    ki = iota((256, D), 0) & 127
    head = head_of(iota((1, D), 1))
    for a in range(LATENT):
        spread[a] = one_hot(ki == a * HEADS + head)

    def gather_slots(half):
        for d in range(8):
            part = fy[half, d].astype(F32)
            whole[d, :, 0:512] = part
            whole[d, :, 512:] = jnp.concatenate(
                [part[12:16, 0:128], part[12:16, 128:256], part[12:16, 256:384], jnp.zeros((4, 128), F32)], axis=0
            )

    def keep(half, pick):
        kept[...] = dot(pick, whole[...].astype(BF16).reshape(128, UNITS))
        for e in range(8):
            fs[8 * half + e] = jnp.concatenate(
                [kept[16 * u : 16 * u + 16, e * IN : (e + 1) * IN] for u in range(4)] + [blank], axis=1
            ).astype(BF16)

    loop(1, 8, lambda t: fy_copy(t, 1).wait_recv())
    loop(1, 8, lambda t: fy_copy(t, 0).start())
    blank = jnp.zeros((16, 64), F32)
    at_row = iota((16, 128), 0)
    at_lane = iota((16, 128), 1)
    picks = []
    for d in range(8):
        listed = fy[1, d, :, 384:512].astype(F32)[12:13]
        level = jnp.sum(jnp.where(at_row == at_lane, listed, 0.0), axis=1, keepdims=True)
        picks.append(
            jnp.where(
                (level == (at_lane % 16).astype(F32)) & (at_row < 12)
                & (at_lane // 32 == d // 4) & (at_row % 2 == (at_lane // 16) % 2),
                1.0,
                0.0,
            )
        )
    pick = jnp.transpose(jnp.concatenate(picks, axis=0))[:64].astype(BF16)
    gather_slots(1)
    keep(1, pick)
    loop(0, 8, lambda k: fz_copy(NZ - 1 - k).start())
    loop(1, 8, lambda k: wz_copy(k).wait_recv())
    regroup(0)
    loop(1, NY, lambda t: near_y(t).start())
    loop(8, NZ, lambda k: wz_copy(k).wait_recv())
    regroup(1)
    loop(1, NX, lambda t: far_x(t).start())
    loop(1, NY, lambda t: wq_copy(t).start())
    loop(1, NY, lambda t: wy_copy(t).start())
    loop(1, 8, lambda t: fy_copy(t, 0).wait_recv())
    gather_slots(0)
    keep(0, pick)
    loop(1, 8, lambda k: fz_copy(8 - k).start())
    fz[z] = fs[0]
    loop(1, NY, lambda t: near_y(t).wait_recv())
    loop(1, NX, lambda t: near_x(t).start())
    loop(1, NX, lambda t: far_x(t).wait_recv())
    loop(1, NY, lambda t: far_y(t).start())
    loop(1, NY, lambda t: wq_copy(t).wait_recv())
    wc_copy(3, c).start()
    loop(1, NY, lambda t: wy_copy(t).wait_recv())
    loop(1, NX, lambda t: wx_copy(t).start())
    loop(1, NX, lambda t: near_x(t).wait_recv())
    wc_copy(0, c).start()

    loop(1, NZ, lambda k: fz_copy(k).wait_recv())
    r = iota((ROWS, 256), 0)
    j = iota((ROWS, 256), 1)
    rows = dot(one_hot(j == (r % 16) * 16 + r // 16), fz[...].reshape(256, 384)).astype(BF16)
    encoding = jnp.broadcast_to(encode[...].astype(F32)[:, None, :], (LEVELS, 16, D)).reshape(ROWS, D)
    for u, (lo, hi) in enumerate(((0, 128), (0, 256), (128, 256), (128, 384))):
        emb[u] = (dot(rows[:, lo:hi], shifted[u, : hi - lo, :]) + encoding).astype(BF16)

    loop(1, NY, lambda t: far_y(t).wait_recv())
    wc_copy(1, c).start()
    scale = 1.0 / math.sqrt(D // HEADS)

    def attend(half):
        g = iota((256, 128), 0) + 256 * half
        at_lane = iota((256, 128), 1)
        qv = q_all[half].astype(F32).reshape(256, 128)
        found = jnp.zeros((256, 128), F32)
        for a in range(LATENT):
            found = jnp.where(at_lane == a * HEADS + head_of(g), qv[:, a : a + 1], found)
        found = found.astype(BF16)
        k_w = w_kv[half, 0].reshape(256, D)
        v_w = w_kv[half, 1].reshape(256, D)
        cut_at = slice(256 * half, 256 * half + 256)
        rows = emb[...].reshape(4 * ROWS, D)
        keys = nt(rows, k_w).astype(BF16)
        scores = (dot(keys, found) * scale).reshape(4, LEVELS, 16, 128)
        highest = jnp.max(scores, axis=1, keepdims=True)
        expo = jnp.exp(scores - highest)
        weight = (expo * (1.0 / jnp.sum(expo, axis=1, keepdims=True))).reshape(4 * ROWS, 128)
        top = weight.astype(BF16)
        low = (weight - top.astype(F32)).astype(BF16)
        both = jnp.concatenate([top, low], axis=1)
        values = nt(rows, v_w).astype(BF16).astype(F32)
        for a in range(LATENT):
            wide = dot(both, spread[a, :, cut_at])
            total = jnp.sum((wide * values).reshape(4, LEVELS, 16, 256), axis=1)
            for u in range(4):
                mixed[a, 2 * half, pl.ds(u, 16, 4), :] = total[u, :, :128]
                mixed[a, 2 * half + 1, pl.ds(u, 16, 4), :] = total[u, :, 128:]

    wc_copy(3, 1 - c).wait_recv()
    wc_copy(0, 1 - c).wait_recv()
    attend(0)
    loop(1, NX, lambda t: wx_copy(t).wait_recv())
    wc_copy(2, c).start()
    wc_copy(1, 1 - c).wait_recv()
    attend(1)
    block = jnp.concatenate(
        [jnp.concatenate([mixed[a, i] for i in range(4)], axis=1) for a in range(LATENT)], axis=0
    ).astype(BF16)
    block = dot(block, natural_t[...]).astype(BF16)
    wc_copy(2, 1 - c).wait_recv()
    block = nt(block, w_o[...].reshape(D, D)).astype(BF16)
    out[...] = dot(block, natural_t[...]).astype(BF16).reshape(LATENT, 64, D)

    loop(1, NZ, lambda k: wz_copy(k).wait_send())
    loop(1, NZ, lambda k: fz_copy(k).wait_send())
    for half in range(2):
        loop(1, 8, lambda t: fy_copy(t, half).wait_send())
    loop(1, NY, lambda t: near_y(t).wait_send())
    loop(1, NX, lambda t: near_x(t).wait_send())
    loop(1, NX, lambda t: far_x(t).wait_send())
    loop(1, NY, lambda t: far_y(t).wait_send())
    loop(1, NY, lambda t: wq_copy(t).wait_send())
    loop(1, NY, lambda t: wy_copy(t).wait_send())
    loop(1, NX, lambda t: wx_copy(t).wait_send())
    for i in range(4):
        wc_copy(i, c).wait_send()


def encode_patches(*operands):
    dma = pltpu.SemaphoreType.DMA
    vmem = pltpu.VMEM
    fields, slot_level, latent, qkv, out_w, embed, encode = operands
    operands = [pltpu.with_memory_space_constraint(o, pltpu.HBM) for o in operands]
    return pl.pallas_call(
        kernel,
        out_shape=jax.ShapeDtypeStruct((LATENT, 64, D), BF16),
        in_specs=[pl.BlockSpec(memory_space=pltpu.HBM)] * 7,
        out_specs=pl.BlockSpec(memory_space=pltpu.VMEM),
        scratch_shapes=[
            vmem(fields.shape, BF16),
            pltpu.SMEM(slot_level.shape, jnp.int32),
            vmem(latent.shape, BF16),
            vmem(qkv.shape, BF16),
            vmem(out_w.shape, BF16),
            vmem(embed.shape, BF16),
            vmem(encode.shape, BF16),
            vmem((NX, 16, 128), BF16),
            vmem((NZ, 16, 128), BF16),
            vmem((2, 4, 2, 16, 128), BF16),
            vmem((2, 2, NC, NY, 2, 16, D), BF16),
            vmem((2, NC, NY, 2, 16, D), BF16),
            vmem((2, NC, NY, 2, 16, 128), BF16),
            vmem((2, 8, 16, 512), BF16),
            vmem((2, 8, 16, 512), BF16),
            vmem((8, 16, UNITS), F32),
            vmem((64, UNITS), F32),
            vmem((NZ, 16, 384), BF16),
            vmem((NZ, 16, 384), BF16),
            vmem((4, 256, D), BF16),
            vmem((4, ROWS, D), BF16),
            vmem((LATENT, 256, D), BF16),
            vmem((D, D), BF16),
            vmem((LATENT, 4, 64, 128), F32),
            dma((7,)),
            dma((NZ,)), dma((NZ,)),
            dma((4, 4)), dma((4, 4)),
            dma((2, NY)), dma((2, NY)),
            dma((NX,)), dma((NX,)),
            dma((4,)), dma((4,)),
            dma((2, 8)), dma((2, 8)),
            dma((NZ,)), dma((NZ,)),
        ],
        compiler_params=pltpu.CompilerParams(
            collective_id=0, has_side_effects=True, vmem_limit_bytes=VMEM_LIMIT
        ),
        cost_estimate=pl.CostEstimate(flops=3 * 10**9, bytes_accessed=10**6, transcendentals=10**5),
        name="encode_patches",
    )(*operands)


def on_device(fields, slot_level, embed_weight, level_encoding, latent_queries, qkv_weight, out_weight):
    out = encode_patches(
        fields, slot_level, latent_queries, qkv_weight, out_weight, embed_weight, level_encoding
    )
    return out.reshape(LATENT, 1, 64, D)


def solution(mesh):
    in_specs = (
        P("lev", "lon", "lat"),
        P("lev"),
        P(),
        P(),
        P(),
        P(None, ("lon", "lev"), None),
        P(("lon", "lev"), None),
    )
    out_specs = P(None, ("lat", "lon", "lev"), None, None)
    return jax.shard_map(
        on_device, mesh=mesh, in_specs=in_specs, out_specs=out_specs, check_vma=False
    )
```

time: 45.2 us -> 41 us (0.907)
  Pallas kernels: 43.1 us -> 40.1 us
  local copies, waits for them, and re-layouts: 1.62 us -> 0.68 us
    pallas_call x1, Pallas kernels: 43.1 us -> 40.1 us  [encode_patches(): pl.pallas_call(kernel, out_shape=jax.ShapeDtypeStruct((LATENT, 64, D), BF...]
    unnamed x1, local copies, waits for them, and re-layouts: 1.62 us -> 0.68 us
where the time goes in v3:
time: 41 us; the launch traced here: 40.8 us
  Pallas kernels  40.1 us (98%)
  local copies, waits for them, and re-layouts  0.68 us (2%)
    pallas_call x1, Pallas kernels, encode_patches(): pl.pallas_call(kernel, out_shape=jax.ShapeDtypeStruct((LATENT, 64, D), BF...  40.1 us

profile of v3, /device:TPU:1, one launch (start us, length us, event | category | flops | bytes accessed | tf_op | source)
XLA Modules:
  0.0 40.8 jit_solution(4082601607351454929)
XLA Ops:
  0.0 40.1 %encode_patches.1 = bf16[3,64,512]{2,1,0:T(8,128)(2,1)S(1)} custom-call(bf16[6,2,10240]{2,1,0:T(2,128)(2,1)} %fields_h.1, s32[6]{0:T(128)} %slot_h.1, bf16[3,512]{1,0:T(4,128)(2,1)} %latent_h.1, bf16[3,4,512]{2,1,0:T(4,128)(2,1)} %qkv_h.1, bf16[4,512]{1,0:T(4,128)(2,1)} %out_w_h.1, bf16[80,512]{1,0:T(8,128)(2,1)} %embed_h.1, bf16[14,512]{1,0:T(8,128)(2,1)} %encode_h.1), custom_call_target="tpu_custom_call" | custom-call | flops 3000000000 | bytes 1000000 | tf_op jit(solution)/shard_map/encode_patches/pallas_call | solution.py:352
  40.1 0.7 %copy.10 = bf16[3,1,64,512]{3,2,1,0:T(8,128)(2,1)} copy(bf16[3,1,64,512]{3,2,1,0:T(8,128)(2,1)S(1)} %bitcast.3) | data formatting | bytes 393216

commit v4 on v3

--- a/solution.py
+++ b/solution.py
@@ -229,6 +229,9 @@
                 [kept[16 * u : 16 * u + 16, e * IN : (e + 1) * IN] for u in range(4)] + [blank], axis=1
             ).astype(BF16)
 
+    loop(1, 8, lambda k: wz_copy(k).wait_recv())
+    regroup(0)
+    loop(1, NY, lambda t: near_y(t).start())
     loop(1, 8, lambda t: fy_copy(t, 1).wait_recv())
     loop(1, 8, lambda t: fy_copy(t, 0).start())
     blank = jnp.zeros((16, 64), F32)
@@ -250,21 +253,18 @@
     gather_slots(1)
     keep(1, pick)
     loop(0, 8, lambda k: fz_copy(NZ - 1 - k).start())
-    loop(1, 8, lambda k: wz_copy(k).wait_recv())
-    regroup(0)
-    loop(1, NY, lambda t: near_y(t).start())
     loop(8, NZ, lambda k: wz_copy(k).wait_recv())
     regroup(1)
     loop(1, NX, lambda t: far_x(t).start())
     loop(1, NY, lambda t: wq_copy(t).start())
     loop(1, NY, lambda t: wy_copy(t).start())
+    loop(1, NY, lambda t: near_y(t).wait_recv())
+    loop(1, NX, lambda t: near_x(t).start())
     loop(1, 8, lambda t: fy_copy(t, 0).wait_recv())
     gather_slots(0)
     keep(0, pick)
     loop(1, 8, lambda k: fz_copy(8 - k).start())
     fz[z] = fs[0]
-    loop(1, NY, lambda t: near_y(t).wait_recv())
-    loop(1, NX, lambda t: near_x(t).start())
     loop(1, NX, lambda t: far_x(t).wait_recv())
     loop(1, NY, lambda t: far_y(t).start())
     loop(1, NY, lambda t: wq_copy(t).wait_recv())
@@ -274,6 +274,8 @@
     loop(1, NX, lambda t: near_x(t).wait_recv())
     wc_copy(0, c).start()
 
+    loop(1, NY, lambda t: far_y(t).wait_recv())
+    wc_copy(1, c).start()
     loop(1, NZ, lambda k: fz_copy(k).wait_recv())
     r = iota((ROWS, 256), 0)
     j = iota((ROWS, 256), 1)
@@ -282,8 +284,6 @@
     for u, (lo, hi) in enumerate(((0, 128), (0, 256), (128, 256), (128, 384))):
         emb[u] = (dot(rows[:, lo:hi], shifted[u, : hi - lo, :]) + encoding).astype(BF16)
 
-    loop(1, NY, lambda t: far_y(t).wait_recv())
-    wc_copy(1, c).start()
     scale = 1.0 / math.sqrt(D // HEADS)
 
     def attend(half):

time: 41 us -> 40 us (0.976)
  Pallas kernels: 40.1 us -> 39.1 us
    pallas_call x1, Pallas kernels: 40.1 us -> 39.1 us  [encode_patches(): pl.pallas_call(kernel, out_shape=jax.ShapeDtypeStruct((LATENT, 64, D), BF...]
where the time goes in v4:
time: 40 us; the launch traced here: 39.8 us
  Pallas kernels  39.1 us (98%)
  local copies, waits for them, and re-layouts  0.68 us (2%)
    pallas_call x1, Pallas kernels, encode_patches(): pl.pallas_call(kernel, out_shape=jax.ShapeDtypeStruct((LATENT, 64, D), BF...  39.1 us

profile of v4, /device:TPU:1, one launch (start us, length us, event | category | flops | bytes accessed | tf_op | source)
XLA Modules:
  0.0 39.8 jit_solution(18419405490311579904)
XLA Ops:
  0.0 39.1 %encode_patches.1 = bf16[3,64,512]{2,1,0:T(8,128)(2,1)S(1)} custom-call(bf16[6,2,10240]{2,1,0:T(2,128)(2,1)} %fields_h.1, s32[6]{0:T(128)} %slot_h.1, bf16[3,512]{1,0:T(4,128)(2,1)} %latent_h.1, bf16[3,4,512]{2,1,0:T(4,128)(2,1)} %qkv_h.1, bf16[4,512]{1,0:T(4,128)(2,1)} %out_w_h.1, bf16[80,512]{1,0:T(8,128)(2,1)} %embed_h.1, bf16[14,512]{1,0:T(8,128)(2,1)} %encode_h.1), custom_call_target="tpu_custom_call" | custom-call | flops 3000000000 | bytes 1000000 | tf_op jit(solution)/shard_map/encode_patches/pallas_call | solution.py:352
  39.1 0.7 %copy.10 = bf16[3,1,64,512]{3,2,1,0:T(8,128)(2,1)} copy(bf16[3,1,64,512]{3,2,1,0:T(8,128)(2,1)S(1)} %bitcast.3) | data formatting | bytes 393216

commit v5 on v4

--- a/solution.py
+++ b/solution.py
@@ -314,11 +314,11 @@
                 mixed[a, 2 * half, pl.ds(u, 16, 4), :] = total[u, :, :128]
                 mixed[a, 2 * half + 1, pl.ds(u, 16, 4), :] = total[u, :, 128:]
 
+    loop(1, NX, lambda t: wx_copy(t).wait_recv())
+    wc_copy(2, c).start()
     wc_copy(3, 1 - c).wait_recv()
     wc_copy(0, 1 - c).wait_recv()
     attend(0)
-    loop(1, NX, lambda t: wx_copy(t).wait_recv())
-    wc_copy(2, c).start()
     wc_copy(1, 1 - c).wait_recv()
     attend(1)
     block = jnp.concatenate(

time: 40 us -> 39.8 us (level)
  no operation moved by 1% of the time
where the time goes in v5:
time: 39.8 us; the launch traced here: 39.7 us
  Pallas kernels  39 us (98%)
  local copies, waits for them, and re-layouts  0.68 us (2%)
    pallas_call x1, Pallas kernels, encode_patches(): pl.pallas_call(kernel, out_shape=jax.ShapeDtypeStruct((LATENT, 64, D), BF...  39 us

profile of v5, /device:TPU:1, one launch (start us, length us, event | category | flops | bytes accessed | tf_op | source)
XLA Modules:
  0.0 39.7 jit_solution(5725863149356467352)
XLA Ops:
  0.0 39.0 %encode_patches.1 = bf16[3,64,512]{2,1,0:T(8,128)(2,1)S(1)} custom-call(bf16[6,2,10240]{2,1,0:T(2,128)(2,1)} %fields_h.1, s32[6]{0:T(128)} %slot_h.1, bf16[3,512]{1,0:T(4,128)(2,1)} %latent_h.1, bf16[3,4,512]{2,1,0:T(4,128)(2,1)} %qkv_h.1, bf16[4,512]{1,0:T(4,128)(2,1)} %out_w_h.1, bf16[80,512]{1,0:T(8,128)(2,1)} %embed_h.1, bf16[14,512]{1,0:T(8,128)(2,1)} %encode_h.1), custom_call_target="tpu_custom_call" | custom-call | flops 3000000000 | bytes 1000000 | tf_op jit(solution)/shard_map/encode_patches/pallas_call | solution.py:352
  39.0 0.7 %copy.10 = bf16[3,1,64,512]{3,2,1,0:T(8,128)(2,1)} copy(bf16[3,1,64,512]{3,2,1,0:T(8,128)(2,1)S(1)} %bitcast.3) | data formatting | bytes 393216

commit v6 on v5

--- a/solution.py
+++ b/solution.py
@@ -308,7 +308,21 @@
         both = jnp.concatenate([top, low], axis=1)
         values = nt(rows, v_w).astype(BF16).astype(F32)
         for a in range(LATENT):
-            wide = dot(both, spread[a, :, cut_at])
+            if a < 2:
+                wide = dot(both, spread[a, :, cut_at])
+            else:
+                wide = jnp.concatenate(
+                    [
+                        jnp.take_along_axis(
+                            weight,
+                            head_of(iota((4 * ROWS, 128), 1) + 256 * half + 128 * i) + a * HEADS,
+                            axis=1,
+                            mode="promise_in_bounds",
+                        )
+                        for i in range(2)
+                    ],
+                    axis=1,
+                )
             total = jnp.sum((wide * values).reshape(4, LEVELS, 16, 256), axis=1)
             for u in range(4):
                 mixed[a, 2 * half, pl.ds(u, 16, 4), :] = total[u, :, :128]

time: 39.8 us -> 39.4 us (0.990)
  Pallas kernels: 39 us -> 38.6 us
    pallas_call x1, Pallas kernels: 39 us -> 38.6 us  [encode_patches(): pl.pallas_call(kernel, out_shape=jax.ShapeDtypeStruct((LATENT, 64, D), BF...]
where the time goes in v6:
time: 39.4 us; the launch traced here: 39.3 us
  Pallas kernels  38.6 us (98%)
  local copies, waits for them, and re-layouts  0.68 us (2%)
    pallas_call x1, Pallas kernels, encode_patches(): pl.pallas_call(kernel, out_shape=jax.ShapeDtypeStruct((LATENT, 64, D), BF...  38.6 us

profile of v6, /device:TPU:1, one launch (start us, length us, event | category | flops | bytes accessed | tf_op | source)
XLA Modules:
  0.0 39.3 jit_solution(15937237071952239817)
XLA Ops:
  0.0 38.6 %encode_patches.1 = bf16[3,64,512]{2,1,0:T(8,128)(2,1)S(1)} custom-call(bf16[6,2,10240]{2,1,0:T(2,128)(2,1)} %fields_h.1, s32[6]{0:T(128)} %slot_h.1, bf16[3,512]{1,0:T(4,128)(2,1)} %latent_h.1, bf16[3,4,512]{2,1,0:T(4,128)(2,1)} %qkv_h.1, bf16[4,512]{1,0:T(4,128)(2,1)} %out_w_h.1, bf16[80,512]{1,0:T(8,128)(2,1)} %embed_h.1, bf16[14,512]{1,0:T(8,128)(2,1)} %encode_h.1), custom_call_target="tpu_custom_call" | custom-call | flops 3000000000 | bytes 1000000 | tf_op jit(solution)/shard_map/encode_patches/pallas_call | solution.py:366
  38.6 0.7 %copy.10 = bf16[3,1,64,512]{3,2,1,0:T(8,128)(2,1)} copy(bf16[3,1,64,512]{3,2,1,0:T(8,128)(2,1)S(1)} %bitcast.3) | data formatting | bytes 393216
